TPU v7x, 32 devices: a whole 2x2x4 slice. The times are simulated.
32 devices in a mesh: param: 8 (over z, x), sensor: 4 (over y, core).
Axes of the slice: x: 2, y: 2, z: 4, core: 2. Of those that a mesh axis runs over, the one named last changes fastest.
Arguments:
- readings: bfloat16 [64, 600, 128], P('param', 'sensor'), may hold values from -6 to 6
- spectra: bfloat16 [2, 65, 600, 1024], P(None, None, 'sensor', 'param'), may hold values from -0.1875 to 0.1875
- stiffness: float32 [1024], P('param'), may hold values from 0.04 to 0.24
Outputs:
- hessian_panel: float32 [64, 600, 128], P('param', 'sensor')
All inputs are finite; a program needn't handle non-finite values.
Results may differ from a plain program's by a relative error of at most 0.0025.
Values may be sent and summed in bfloat16 or wider, within the bound.
A program may use at most 128 MiB of HBM per device.

v0:
```python
import functools
import math

import jax
import jax.numpy as jnp
import ml_dtypes
import numpy as np
from jax import lax
from jax.experimental import pallas as pl
from jax.experimental.pallas import tpu as pltpu
from jax.sharding import PartitionSpec as P_

STEPS = 64
GY = 64
NCOL = 128


def with_halo(block, sides, width):
    for axis, dim in sides:
        count = lax.axis_size(axis)
        forward = [(i, i + 1) for i in range(count - 1)]
        backward = [(target, source) for source, target in forward]
        low = lax.ppermute(
            lax.slice_in_dim(block, block.shape[dim] - width, None, axis=dim), axis, forward
        )
        high = lax.ppermute(lax.slice_in_dim(block, 0, width, axis=dim), axis, backward)
        block = jnp.concatenate([low, block, high], axis=dim)
    return block


def angles(bins, times):
    prod = bins[:, None] * times[None, :] % (2 * STEPS)
    return prod.astype(jnp.float32) * (2.0 * math.pi / (2 * STEPS))


def accumulate(loop_carry, piece):
    count = piece.shape[0]
    bins = jnp.arange(STEPS + 1, dtype=jnp.int32)
    times = jnp.arange(count, dtype=jnp.int32)
    phase_angle = angles(bins, times)
    scale_factor = 1.0 / math.sqrt(STEPS)
    value_entries = piece.astype(jnp.float32)
    hessian_product = lax.Precision.HIGHEST
    real_part = jnp.einsum(
        "uo,ojm->ujm", jnp.cos(phase_angle) * scale_factor, value_entries, precision=hessian_product
    )
    imaginary_part = loop_carry[1] - jnp.einsum(
        "uo,ojm->ujm", jnp.sin(phase_angle) * scale_factor, value_entries, precision=hessian_product
    )
    return (real_part, imaginary_part)


def inverse_rows(real_part, imaginary_part, count):
    bins = jnp.arange(STEPS + 1, dtype=jnp.int32)
    times = jnp.arange(count, dtype=jnp.int32)
    phase_angle = angles(bins, times)
    weight = jnp.where((bins == 0) | (bins == STEPS), 1.0, 2.0).astype(jnp.float32)[:, None]
    scale_factor = 1.0 / math.sqrt(STEPS)
    hessian_product = lax.Precision.HIGHEST
    cosine_inverse = (jnp.cos(phase_angle) * weight * scale_factor).T
    sine_inverse = (jnp.sin(phase_angle) * weight * scale_factor).T
    return jnp.einsum(
        "ni,ilj->nlj", cosine_inverse, real_part, precision=hessian_product
    ) - jnp.einsum("ni,ilj->nlj", sine_inverse, imaginary_part, precision=hessian_product)


def sweep_once(grid, coeff):
    padded = with_halo(grid.astype(jnp.bfloat16), (("param", 1),), 1).astype(grid.dtype)
    sides = jnp.pad(grid, ((0, 0), (0, 0), (1, 1), (0, 0)))
    beside_all = padded[:, :-2] + padded[:, 2:] + sides[:, :, :-2] + sides[:, :, 2:]
    return grid + coeff * (beside_all - 4.0 * grid)


def shards(readings, spectra, stiffness):
    sens_rows = readings.shape[1]
    points = spectra.shape[3]
    rows_here = points // GY
    empty_data = jnp.zeros((STEPS + 1, sens_rows, NCOL), jnp.float32)
    data_re, data_im = accumulate(
        (empty_data, empty_data), lax.all_gather(readings, "param", axis=0, tiled=True)
    )
    data_re = data_re.astype(jnp.bfloat16)
    data_im = data_im.astype(jnp.bfloat16)
    spectrum_real = spectra[0]
    spectrum_imaginary = spectra[1]
    f32 = jnp.float32
    adj_re = jnp.einsum(
        "ksm,ksc->kmc", spectrum_real, data_re, preferred_element_type=f32
    ) + jnp.einsum("ksm,ksc->kmc", spectrum_imaginary, data_im, preferred_element_type=f32)
    adj_im = jnp.einsum(
        "ksm,ksc->kmc", spectrum_real, data_im, preferred_element_type=f32
    ) - jnp.einsum("ksm,ksc->kmc", spectrum_imaginary, data_re, preferred_element_type=f32)
    field = inverse_rows(adj_re, adj_im, STEPS)
    grid = field.reshape(STEPS, rows_here, GY, NCOL)
    coeff = stiffness.reshape(rows_here, GY)[None, :, :, None]
    empty_model = jnp.zeros((STEPS + 1, points, NCOL), jnp.float32)
    share = lax.psum_scatter(grid, "sensor", scatter_dimension=0, tiled=True)
    for sweep in range(2):
        share = sweep_once(share, coeff)
    flat = share.reshape(share.shape[0], points, NCOL)
    model_re, model_im = accumulate(
        (empty_model, empty_model), lax.all_gather(flat, "sensor", axis=0, tiled=True)
    )
    model_re = model_re.astype(jnp.bfloat16)
    model_im = model_im.astype(jnp.bfloat16)
    out_re = jnp.einsum(
        "ksm,kmc->ksc", spectrum_real, model_re, preferred_element_type=f32
    ) - jnp.einsum("ksm,kmc->ksc", spectrum_imaginary, model_im, preferred_element_type=f32)
    out_im = jnp.einsum(
        "ksm,kmc->ksc", spectrum_real, model_im, preferred_element_type=f32
    ) + jnp.einsum("ksm,kmc->ksc", spectrum_imaginary, model_re, preferred_element_type=f32)
    return lax.psum_scatter(
        inverse_rows(out_re, out_im, readings.shape[0] * lax.axis_size("param")),
        "param",
        scatter_dimension=0,
        tiled=True,
    )


MESH = pl.DeviceIdType.MESH
BF = jnp.bfloat16
F32 = jnp.float32


def split16(table):
    high = table.astype(np.float32).astype(ml_dtypes.bfloat16)
    low = (table - high.astype(np.float64)).astype(np.float32).astype(ml_dtypes.bfloat16)
    return high, low


def tables(params, held):
    bins = STEPS + 1
    rows = -(-bins // 8) * 8
    angle = 2.0 * np.pi * (np.outer(np.arange(bins), np.arange(STEPS)) % (2 * STEPS)) / (2 * STEPS)
    weight = np.where(np.isin(np.arange(bins), (0, STEPS)), 1.0, 2.0)[:, None]
    forward = np.zeros((2, rows, STEPS))
    forward[0, :bins] = np.cos(angle) / math.sqrt(STEPS)
    forward[1, :bins] = -np.sin(angle) / math.sqrt(STEPS)
    inverse = forward.copy()
    inverse[:, :bins] *= weight
    forward = forward.reshape(2 * rows, STEPS)
    inverse = inverse.reshape(2 * rows, STEPS).T
    pair = np.zeros((2, 2 * rows, params, 2, held))
    for one in range(2):
        pair[one, :, :, one, :] = forward.reshape(2 * rows, params, held)
    pair = pair.reshape(4 * rows, 2 * STEPS)
    pair_high, pair_low = split16(pair)
    fwd_high, fwd_low = split16(forward)
    inv_high, inv_low = split16(inverse)
    return (
        rows,
        np.concatenate([pair_high, pair_low], 1),
        np.concatenate([fwd_high, fwd_low], 1),
        np.concatenate([inv_high, inv_high, inv_low], 1),
    )


def best_unroll(count, choices):
    return next(u for u in choices if count % u == 0)


def remote(src, dst, send, recv, param, sensor):
    return pltpu.make_async_remote_copy(
        src_ref=src, dst_ref=dst, send_sem=send, recv_sem=recv,
        device_id=(param, sensor), device_id_type=MESH,
    )


def dot(a, b):
    return jnp.dot(a, b, preferred_element_type=F32)


def dot_rows(a, b):
    return lax.dot_general(a, b, (((0,), (0,)), ((), ())), preferred_element_type=F32)


def by_chunks(total, step, body):
    def one(i, carry):
        body(pl.ds(pl.multiple_of(i * step, step), step))
        return carry

    lax.fori_loop(0, total // step, one, 0)


def three(x):
    high = x.astype(BF)
    low = (x - high.astype(F32)).astype(BF)
    return jnp.concatenate([high, low, high], 0)


def kernel(cfg, own_ref, spec_ref, stiff_ref, pair_ref, fwd_ref, inv_ref, out_ref,
           rg, dre, dim, are, aim, fq, cr, ys, yr, sh, sh2, hb, hl, hh, sg, ob, xr, us, ds, ur, dr,
           a_xs, a_xr, a_us, a_ds, a_zr, c_s, c_r, y_s, y_r, h_s, h_r, e_s, e_r,
           x_s, x_r, u_s, u_r, d_s, d_r):
    P, S, sens, rows, R = cfg
    Z = P // 2
    bins = STEPS + 1
    stride = dre.shape[0] // rows
    points = are.shape[0] // rows
    T = STEPS // S
    held = STEPS // P
    block = own_ref.shape[0]
    p, q = lax.axis_index("param"), lax.axis_index("sensor")
    x, z = lax.rem(p, 2), p // 2
    xp = p + 1 - 2 * x
    core, y = lax.rem(q, 2), q // 2
    qc = y * 2 + 1 - core
    qy = (1 - y) * 2 + core
    above, below = z < Z - 1, z > 0
    odd_up = (x == 1) & (p < P - 1)
    odd_dn = (x == 0) & (p > 0)

    barrier = pltpu.get_barrier_semaphore()
    partners = ((None, xp, q), (None, p, qc), (None, p, qy), (above, p + 2, q), (below, p - 2, q),
                (odd_up, p + 1, q), (odd_dn, p - 1, q))

    def maybe(cond, f):
        if cond is None:
            f()
        else:
            pl.when(cond)(f)

    for cond, dp, dq in partners:
        maybe(cond, lambda dp=dp, dq=dq: pl.semaphore_signal(barrier, inc=1, device_id=(dp, dq), device_id_type=MESH))
    count = jnp.int32(0)
    for cond, _, _ in partners:
        count = count + (1 if cond is None else jnp.where(cond, 1, 0))
    pl.semaphore_wait(barrier, count)

    def up_copy(d):
        src = own_ref if d == 0 else rg.at[p - 2 * d]
        return remote(src, rg.at[p - 2 * d], a_us.at[d], a_zr.at[z - d], p + 2, q)

    def dn_copy(d):
        src = own_ref if d == 0 else rg.at[p + 2 * d]
        return remote(src, rg.at[p + 2 * d], a_ds.at[d], a_zr.at[z + d], p - 2, q)

    def x_copy(origin):
        return remote(rg.at[origin * 2 + x], rg.at[origin * 2 + x], a_xs.at[origin], a_xr.at[origin], xp, q)

    pl.when(above)(lambda: up_copy(0).start())
    pl.when(below)(lambda: dn_copy(0).start())
    rg[p] = own_ref[...]
    x_copy(z).start()
    for k in range(bins, rows):
        are[k * points:(k + 1) * points, :] = jnp.zeros((points, NCOL), F32)
        aim[k * points:(k + 1) * points, :] = jnp.zeros((points, NCOL), F32)
    for d in range(1, Z):
        @pl.when(z >= d)
        def _():
            remote(rg.at[p - 2 * d], rg.at[p - 2 * d], a_us.at[d], a_zr.at[z - d], p, q).wait_recv()
            pl.when(above)(lambda: up_copy(d).start())
            x_copy(z - d).start()

        @pl.when(z + d < Z)
        def _():
            remote(rg.at[p + 2 * d], rg.at[p + 2 * d], a_ds.at[d], a_zr.at[z + d], p, q).wait_recv()
            pl.when(below)(lambda: dn_copy(d).start())
            x_copy(z + d).start()
    for o in range(Z):
        c = remote(rg.at[o * 2 + 1 - x], rg.at[o * 2 + 1 - x], a_xs.at[o], a_xr.at[o], xp, q)
        c.wait_recv()
    for d in range(Z):
        pl.when(above & (z >= d))(lambda: up_copy(d).wait_send())
        pl.when(below & (z + d < Z))(lambda: dn_copy(d).wait_send())
        x_copy(d).wait_send()

    pairs = sens // 2
    u = best_unroll(pairs, (5, 4, 3, 2, 1))

    def data_pairs(i, carry):
        parts = []
        for j in range(u):
            at = pl.ds(pl.multiple_of((i * u + j) * 16, 16), 16)
            parts.append(jnp.concatenate([rg[k, at, :] for k in range(P)], 0))
        block_in = jnp.concatenate(parts, 1)
        both = dot(pair_ref[...], jnp.concatenate([block_in, block_in], 0))
        for j in range(u):
            for one in range(2):
                at = pl.ds((i * u + j) * 2 + one, rows, stride)
                cols = slice(j * NCOL, (j + 1) * NCOL)
                top = one * 2 * rows
                dre[at, :] = both[top:top + rows, cols]
                dim[at, :] = both[top + rows:top + 2 * rows, cols]
        return carry

    lax.fori_loop(0, pairs // u, data_pairs, 0)

    def adjoint(f, carry):
        at = pl.ds(pl.multiple_of(f * stride, 8), sens)
        real, imag = dre[at, :].astype(BF), dim[at, :].astype(BF)
        got = dot_rows(spec_ref[0, f], jnp.concatenate([real, imag], 1))
        got = got + dot_rows(spec_ref[1, f], jnp.concatenate([imag, -real], 1))
        to = pl.ds(pl.multiple_of(f * points, 8), points)
        are[to, :] = got[:, :NCOL]
        aim[to, :] = got[:, NCOL:]
        return carry

    lax.fori_loop(0, bins, adjoint, 0)

    um = best_unroll(points, (4, 2, 1))

    def field_points(i, carry):
        parts = []
        for j in range(um):
            at = pl.ds(i * um + j, rows, points)
            parts.append(jnp.concatenate([are[at, :], aim[at, :]], 0))
        got = dot(inv_ref[...], three(jnp.concatenate(parts, 1)))
        for j in range(um):
            for k in range(S):
                to = pl.ds(pl.multiple_of((i * um + j) * T, T), T)
                fq[k, to, :] = got[k * T:(k + 1) * T, j * NCOL:(j + 1) * NCOL].astype(fq.dtype)
        return carry

    lax.fori_loop(0, points // um, field_points, 0)

    share = points * T
    step = 128

    def c_copy(yy):
        return remote(fq.at[yy * 2 + 1 - core], cr.at[yy], c_s.at[yy], c_r.at[yy], p, qc)

    c_copy(1 - y).start()
    c_copy(y).start()
    c_copy(1 - y).wait_recv()

    def sum_other(at):
        ys[at, :] = (fq[qy, at, :].astype(F32) + cr[1 - y, at, :].astype(F32)).astype(BF)

    by_chunks(share, step, sum_other)
    y_copy = remote(ys, yr, y_s.at[0], y_r.at[0], p, qy)
    y_copy.start()
    c_copy(y).wait_recv()

    def sum_own(at):
        sh[at, :] = fq[q, at, :].astype(F32) + cr[y, at, :].astype(F32)

    by_chunks(share, step, sum_own)
    y_copy.wait_recv()

    def sum_y(at):
        got = sh[at, :] + yr[at, :].astype(F32)
        sh[at, :] = got
        hb[0, at, :] = got.astype(BF)

    by_chunks(share, step, sum_y)

    line = GY * T

    def to_low(s):
        return remote(hb.at[s, pl.ds(0, line)], hh.at[s], h_s.at[s, 0], h_r.at[s, 0], p - 1, q)

    def to_high(s):
        return remote(hb.at[s, pl.ds((R - 1) * line, line)], hl.at[s], h_s.at[s, 1], h_r.at[s, 1], p + 1, q)

    for s in range(2):
        src = sh if s == 0 else sh2
        pl.when(p > 0)(lambda: to_low(s).start())
        pl.when(p < P - 1)(lambda: to_high(s).start())

        @pl.when(p > 0)
        def _():
            to_high(s).wait_recv()

        @pl.when(p == 0)
        def _():
            hl[s] = jnp.zeros((line, NCOL), BF)

        @pl.when(p < P - 1)
        def _():
            to_low(s).wait_recv()

        @pl.when(p == P - 1)
        def _():
            hh[s] = jnp.zeros((line, NCOL), BF)

        def grid_column(g, carry):
            left = jnp.where(g > 0, 1.0, 0.0)
            right = jnp.where(g < GY - 1, 1.0, 0.0)

            def cell(r, c):
                return pl.ds(pl.multiple_of(r * line + c * T, T), T)

            for r in range(R):
                here = src[cell(r, g), :]
                side = left * src[cell(r, jnp.maximum(g - 1, 0)), :]
                side = side + right * src[cell(r, jnp.minimum(g + 1, GY - 1)), :]
                low = hl[s, cell(0, g), :].astype(F32) if r == 0 else src[cell(r - 1, g), :]
                high = hh[s, cell(0, g), :].astype(F32) if r == R - 1 else src[cell(r + 1, g), :]
                new = here + stiff_ref[r * GY + g] * (low + high + side - 4.0 * here)
                if s == 0:
                    sh2[cell(r, g), :] = new
                    hb[1, cell(r, g), :] = new.astype(BF)
                else:
                    sg[q, cell(r, g), :] = new.astype(BF)
            return carry

        lax.fori_loop(0, GY, grid_column, 0)

    e_y = remote(sg.at[q], sg.at[q], e_s.at[0], e_r.at[0], p, qy)
    e_c = remote(sg.at[q], sg.at[q], e_s.at[1], e_r.at[1], p, qc)
    e_f = remote(sg.at[qy], sg.at[qy], e_s.at[2], e_r.at[2], p, qc)
    e_y.start()
    e_c.start()
    remote(sg.at[qy], sg.at[qy], e_s.at[0], e_r.at[0], p, qy).wait_recv()
    e_f.start()
    remote(sg.at[qc], sg.at[qc], e_s.at[1], e_r.at[1], p, qc).wait_recv()
    diag = (1 - y) * 2 + 1 - core
    remote(sg.at[diag], sg.at[diag], e_s.at[2], e_r.at[2], p, qc).wait_recv()

    def model_points(i, carry):
        parts = []
        for j in range(um):
            at = pl.ds(pl.multiple_of((i * um + j) * T, T), T)
            parts.append(jnp.concatenate([sg[k, at, :] for k in range(S)], 0))
        block_in = jnp.concatenate(parts, 1)
        got = dot(fwd_ref[...], jnp.concatenate([block_in, block_in], 0))
        for j in range(um):
            to = pl.ds(i * um + j, rows, points)
            cols = slice(j * NCOL, (j + 1) * NCOL)
            are[to, :] = got[:rows, cols]
            aim[to, :] = got[rows:, cols]
        return carry

    lax.fori_loop(0, points // um, model_points, 0)

    def forward_bin(f, carry):
        at = pl.ds(pl.multiple_of(f * points, 8), points)
        real, imag = are[at, :], aim[at, :]
        model = jnp.concatenate(
            [jnp.concatenate([real, imag], 1), jnp.concatenate([-imag, real], 1)], 0
        )
        high = model.astype(BF)
        low = (model - high.astype(F32)).astype(BF)
        both = jnp.concatenate([spec_ref[0, f], spec_ref[1, f]], 1)
        got = dot(both, high) + dot(both, low)
        to = pl.ds(pl.multiple_of(f * stride, 8), sens)
        dre[to, :] = got[:, :NCOL]
        dim[to, :] = got[:, NCOL:]
        return carry

    lax.fori_loop(0, bins, forward_bin, 0)

    def out_pairs(i, carry):
        parts = []
        for j in range(2 * u):
            at = pl.ds(i * 2 * u + j, rows, stride)
            parts.append(jnp.concatenate([dre[at, :], dim[at, :]], 0))
        got = dot(inv_ref[...], three(jnp.concatenate(parts, 1)))
        for j in range(u):
            to = pl.ds(pl.multiple_of((i * u + j) * 16, 16), 16)
            for k in range(P):
                first = got[k * held:(k + 1) * held, 2 * j * NCOL:(2 * j + 1) * NCOL]
                second = got[k * held:(k + 1) * held, (2 * j + 1) * NCOL:(2 * j + 2) * NCOL]
                ob[k, to, :] = jnp.concatenate([first, second], 0).astype(BF)
        return carry

    lax.fori_loop(0, pairs // u, out_pairs, 0)

    def xo_copy(o):
        return remote(ob.at[o * 2 + 1 - x], xr.at[o], x_s.at[o], x_r.at[o], xp, q)

    order = []
    for k in range(Z // 2):
        order += [Z - 1 - k, k]
    order += [o for o in range(Z) if o not in order]
    for o in order:
        xo_copy(o).start()
    for o in order:
        xo_copy(o).wait_recv()
    cut = 16 * best_unroll(block // 16, (5, 4, 3, 2, 1))

    def mine(o, at):
        return ob[o * 2 + x, at, :].astype(F32) + xr[o, at, :].astype(F32)

    def uo_copy(o):
        return remote(us.at[o], ur.at[o], u_s.at[o], u_r.at[o], p + 2, q)

    def do_copy(o):
        return remote(ds.at[o], dr.at[o], d_s.at[o], d_r.at[o], p - 2, q)

    def pass_on(o, first, buf, got, copy):
        @pl.when(first)
        def _():
            def body(at):
                buf[o, at, :] = mine(o, at)

            by_chunks(block, cut, body)

        @pl.when(jnp.logical_not(first))
        def _():
            copy(o).wait_recv()

            def body(at):
                buf[o, at, :] = mine(o, at) + got[o, at, :]

            by_chunks(block, cut, body)

        copy(o).start()

    for k in range(Z - 1):
        hi, lo = Z - 1 - k, k
        pl.when(z < hi)(lambda: pass_on(hi, z == 0, us, ur, uo_copy))
        pl.when(z > lo)(lambda: pass_on(lo, z == Z - 1, ds, dr, do_copy))

    def total(at):
        out_ref[at, :] = mine(z, at)

    by_chunks(block, cut, total)

    @pl.when(z > 0)
    def _():
        uo_copy(z).wait_recv()

        def body(at):
            out_ref[at, :] += ur[z, at, :]

        by_chunks(block, cut, body)

    @pl.when(z < Z - 1)
    def _():
        do_copy(z).wait_recv()

        def body(at):
            out_ref[at, :] += dr[z, at, :]

        by_chunks(block, cut, body)

    c_copy(0).wait_send()
    c_copy(1).wait_send()
    y_copy.wait_send()
    for s in range(2):
        pl.when(p > 0)(lambda: to_low(s).wait_send())
        pl.when(p < P - 1)(lambda: to_high(s).wait_send())
    e_y.wait_send()
    e_c.wait_send()
    e_f.wait_send()
    for o in range(Z):
        xo_copy(o).wait_send()
        pl.when(z < o)(lambda: uo_copy(o).wait_send())
        pl.when(z > o)(lambda: do_copy(o).wait_send())


def fused(readings, spectra, stiffness):
    P, S = lax.axis_size("param"), lax.axis_size("sensor")
    held, sens, _ = readings.shape
    points = spectra.shape[3]
    R = points // GY
    Z, T = P // 2, STEPS // S
    rows, pair, fwd, inv = tables(P, held)
    stride = -(-sens // 8) * 8
    block = sens * held
    own = readings.transpose(1, 0, 2).reshape(block, NCOL)
    vm = pl.BlockSpec(memory_space=pltpu.VMEM)
    dma = pltpu.SemaphoreType.DMA
    share = points * T
    out = pl.pallas_call(
        functools.partial(kernel, (P, S, sens, rows, R)),
        out_shape=jax.ShapeDtypeStruct((block, NCOL), F32),
        in_specs=[vm, vm, pl.BlockSpec(memory_space=pltpu.SMEM), vm, vm, vm],
        out_specs=vm,
        scratch_shapes=[
            pltpu.VMEM((P, block, NCOL), BF),
            pltpu.VMEM((rows * stride, NCOL), F32),
            pltpu.VMEM((rows * stride, NCOL), F32),
            pltpu.VMEM((rows * points, NCOL), F32),
            pltpu.VMEM((rows * points, NCOL), F32),
            pltpu.VMEM((S, share, NCOL), F32),
            pltpu.VMEM((2, share, NCOL), F32),
            pltpu.VMEM((share, NCOL), BF),
            pltpu.VMEM((share, NCOL), BF),
            pltpu.VMEM((share, NCOL), F32),
            pltpu.VMEM((share, NCOL), F32),
            pltpu.VMEM((2, share, NCOL), BF),
            pltpu.VMEM((2, GY * T, NCOL), BF),
            pltpu.VMEM((2, GY * T, NCOL), BF),
            pltpu.VMEM((S, share, NCOL), BF),
            pltpu.VMEM((P, block, NCOL), BF),
            pltpu.VMEM((Z, block, NCOL), BF),
            pltpu.VMEM((Z, block, NCOL), F32),
            pltpu.VMEM((Z, block, NCOL), F32),
            pltpu.VMEM((Z, block, NCOL), F32),
            pltpu.VMEM((Z, block, NCOL), F32),
            dma((Z,)), dma((Z,)), dma((Z,)), dma((Z,)), dma((Z,)),
            dma((2,)), dma((2,)), dma((1,)), dma((1,)),
            dma((2, 2)), dma((2, 2)), dma((3,)), dma((3,)),
            dma((Z,)), dma((Z,)), dma((Z,)), dma((Z,)), dma((Z,)), dma((Z,)),
        ],
        compiler_params=pltpu.CompilerParams(
            collective_id=0, has_side_effects=True, vmem_limit_bytes=60 * 2**20
        ),
    )(own, spectra, stiffness, jnp.asarray(pair), jnp.asarray(fwd), jnp.asarray(inv))
    return out.reshape(sens, held, NCOL).transpose(1, 0, 2)


def solution(mesh):
    P, S = mesh.shape["param"], mesh.shape["sensor"]
    whole_tiles = P % 2 == 0 and S == 4 and STEPS % (8 * P) == 0
    return jax.shard_map(
        fused if whole_tiles else shards,
        mesh=mesh,
        in_specs=(P_("param", "sensor", None), P_(None, None, "sensor", "param"), P_("param")),
        out_specs=P_("param", "sensor", None),
        check_vma=False,
    )
```

profile of v0, /device:TPU:0, one launch (start us, length us, event | category | flops | bytes accessed | tf_op | source)
XLA Modules:
  0.0 243.2 jit_solution(10511242919532689293)
XLA Ops:
  0.0 5.3 %copy.7.spec_ref = bf16[2,65,150,128]{3,2,1,0:T(8,128)(2,1)} copy(bf16[2,65,150,128]{3,0,2,1:T(2,128)(2,1)} %param.7) | data formatting | bytes 9984000 | tf_op args[1]
  5.3 235.9 %shard_map.64 = f32[1200,128]{1,0:T(8,128)} custom-call(bf16[1200,128]{1,0:T(8,128)(2,1)} %bitcast.7, bf16[2,65,150,128]{3,2,1,0:T(8,128)(2,1)} %copy.7.spec_ref, f32[128]{0:T(128)} %stiff_ref.1, bf16[288,256]{1,0:T(8,128)(2,1)} %constant.6.clone.pair_ref, bf16[144,128]{1,0:T(8,128)(2,1)} %constant.7.clone.fwd_ref, bf16[64,432]{1,0:T(8,128)(2,1)} %constant.8.clone.inv_ref), custom_call_target="tpu_custom_call" | custom-call | tf_op jit(solution)/shard_map/pallas_call | solution.py:557
  241.2 1.9 copy.9
where the time goes:
time: 243 us
  Pallas kernels  236 us (97%)
  local copies, waits for them, and re-layouts  7.22 us (3%)
    pallas_call x1, Pallas kernels, fused(): pl.pallas_call(functools.partial(kernel, (P, S, sens, rows, R)), out_shap...  236 us
    unnamed x2, local copies, waits for them, and re-layouts  7.22 us

commit v1 on v0

--- a/solution.py
+++ b/solution.py
@@ -188,9 +188,9 @@
     return jnp.concatenate([high, low, high], 0)
 
 
-def kernel(cfg, own_ref, spec_ref, stiff_ref, pair_ref, fwd_ref, inv_ref, out_ref,
+def kernel(cfg, own_ref, spec_hbm, stiff_ref, pair_ref, fwd_ref, inv_ref, out_ref,
            rg, dre, dim, are, aim, fq, cr, ys, yr, sh, sh2, hb, hl, hh, sg, ob, xr, us, ds, ur, dr,
-           a_xs, a_xr, a_us, a_ds, a_zr, c_s, c_r, y_s, y_r, h_s, h_r, e_s, e_r,
+           spec_ref, spec_sem, a_xs, a_xr, a_us, a_ds, a_zr, c_s, c_r, y_s, y_r, h_s, h_r, e_s, e_r,
            x_s, x_r, u_s, u_r, d_s, d_r):
     P, S, sens, rows, R = cfg
     Z = P // 2
@@ -227,46 +227,34 @@
         count = count + (1 if cond is None else jnp.where(cond, 1, 0))
     pl.semaphore_wait(barrier, count)
 
-    def up_copy(d):
-        src = own_ref if d == 0 else rg.at[p - 2 * d]
-        return remote(src, rg.at[p - 2 * d], a_us.at[d], a_zr.at[z - d], p + 2, q)
-
-    def dn_copy(d):
-        src = own_ref if d == 0 else rg.at[p + 2 * d]
-        return remote(src, rg.at[p + 2 * d], a_ds.at[d], a_zr.at[z + d], p - 2, q)
-
-    def x_copy(origin):
-        return remote(rg.at[origin * 2 + x], rg.at[origin * 2 + x], a_xs.at[origin], a_xr.at[origin], xp, q)
-
-    pl.when(above)(lambda: up_copy(0).start())
-    pl.when(below)(lambda: dn_copy(0).start())
-    rg[p] = own_ref[...]
-    x_copy(z).start()
-    for k in range(bins, rows):
-        are[k * points:(k + 1) * points, :] = jnp.zeros((points, NCOL), F32)
-        aim[k * points:(k + 1) * points, :] = jnp.zeros((points, NCOL), F32)
-    for d in range(1, Z):
-        @pl.when(z >= d)
-        def _():
-            remote(rg.at[p - 2 * d], rg.at[p - 2 * d], a_us.at[d], a_zr.at[z - d], p, q).wait_recv()
-            pl.when(above)(lambda: up_copy(d).start())
-            x_copy(z - d).start()
-
-        @pl.when(z + d < Z)
-        def _():
-            remote(rg.at[p + 2 * d], rg.at[p + 2 * d], a_ds.at[d], a_zr.at[z + d], p, q).wait_recv()
-            pl.when(below)(lambda: dn_copy(d).start())
-            x_copy(z + d).start()
-    for o in range(Z):
-        c = remote(rg.at[o * 2 + 1 - x], rg.at[o * 2 + 1 - x], a_xs.at[o], a_xr.at[o], xp, q)
-        c.wait_recv()
-    for d in range(Z):
-        pl.when(above & (z >= d))(lambda: up_copy(d).wait_send())
-        pl.when(below & (z + d < Z))(lambda: dn_copy(d).wait_send())
-        x_copy(d).wait_send()
-
     pairs = sens // 2
     u = best_unroll(pairs, (5, 4, 3, 2, 1))
+    rounds = pairs // u
+    NC = best_unroll(rounds, (5, 4, 3, 2, 1))
+    per = rounds // NC
+    CB = block // NC
+
+    spec_copy = pltpu.make_async_copy(spec_hbm, spec_ref, spec_sem)
+    spec_copy.start()
+
+    def piece(c):
+        return pl.ds(c * CB, CB)
+
+    def up_copy(d, c):
+        src = own_ref.at[piece(c)] if d == 0 else rg.at[p - 2 * d, piece(c)]
+        return remote(src, rg.at[p - 2 * d, piece(c)], a_us.at[d, c], a_zr.at[z - d, c], p + 2, q)
+
+    def dn_copy(d, c):
+        src = own_ref.at[piece(c)] if d == 0 else rg.at[p + 2 * d, piece(c)]
+        return remote(src, rg.at[p + 2 * d, piece(c)], a_ds.at[d, c], a_zr.at[z + d, c], p - 2, q)
+
+    def x_copy(d, o, c):
+        at = rg.at[o * 2 + x, piece(c)]
+        return remote(own_ref.at[piece(c)] if d == 0 else at, at, a_xs.at[o, c], a_xr.at[o, c], xp, q)
+
+    def z_arrival(o, c):
+        at = rg.at[o * 2 + x, piece(c)]
+        return remote(at, at, a_us.at[0, c], a_zr.at[o, c], p, q)
 
     def data_pairs(i, carry):
         parts = []
@@ -284,7 +272,47 @@
                 dim[at, :] = both[top + rows:top + 2 * rows, cols]
         return carry
 
-    lax.fori_loop(0, pairs // u, data_pairs, 0)
+    for n in range(NC + Z):
+        if n < NC:
+            pl.when(above)(lambda: up_copy(0, n).start())
+            pl.when(below)(lambda: dn_copy(0, n).start())
+            x_copy(0, z, n).start()
+        if n == 0:
+            rg[p] = own_ref[...]
+            for k in range(bins, rows):
+                are[k * points:(k + 1) * points, :] = jnp.zeros((points, NCOL), F32)
+                aim[k * points:(k + 1) * points, :] = jnp.zeros((points, NCOL), F32)
+        for d in range(1, Z):
+            c = n - d
+            if not 0 <= c < NC:
+                continue
+
+            @pl.when(z >= d)
+            def _():
+                z_arrival(z - d, c).wait_recv()
+                pl.when(above)(lambda: up_copy(d, c).start())
+                x_copy(d, z - d, c).start()
+
+            @pl.when(z + d < Z)
+            def _():
+                z_arrival(z + d, c).wait_recv()
+                pl.when(below)(lambda: dn_copy(d, c).start())
+                x_copy(d, z + d, c).start()
+        c = n - Z
+        if c >= 0:
+            for o in range(Z):
+                at = rg.at[o * 2 + 1 - x, piece(c)]
+                remote(at, at, a_xs.at[o, c], a_xr.at[o, c], xp, q).wait_recv()
+            lax.fori_loop(c * per, (c + 1) * per, data_pairs, 0)
+    for c in range(NC):
+        x_copy(0, z, c).wait_send()
+        for d in range(Z):
+            pl.when(above & (z >= d))(lambda: up_copy(d, c).wait_send())
+            pl.when(below & (z + d < Z))(lambda: dn_copy(d, c).wait_send())
+            if d > 0:
+                pl.when(z >= d)(lambda: x_copy(d, z - d, c).wait_send())
+                pl.when(z + d < Z)(lambda: x_copy(d, z + d, c).wait_send())
+    spec_copy.wait()
 
     def adjoint(f, carry):
         at = pl.ds(pl.multiple_of(f * stride, 8), sens)
@@ -455,76 +483,92 @@
                 ob[k, to, :] = jnp.concatenate([first, second], 0).astype(BF)
         return carry
 
-    lax.fori_loop(0, pairs // u, out_pairs, 0)
-
-    def xo_copy(o):
-        return remote(ob.at[o * 2 + 1 - x], xr.at[o], x_s.at[o], x_r.at[o], xp, q)
+    def xo_copy(o, c):
+        at = piece(c)
+        return remote(ob.at[o * 2 + 1 - x, at], xr.at[o, at], x_s.at[o, c], x_r.at[o, c], xp, q)
 
     order = []
     for k in range(Z // 2):
         order += [Z - 1 - k, k]
     order += [o for o in range(Z) if o not in order]
-    for o in order:
-        xo_copy(o).start()
-    for o in order:
-        xo_copy(o).wait_recv()
-    cut = 16 * best_unroll(block // 16, (5, 4, 3, 2, 1))
+    cut = 16 * best_unroll(CB // 16, (5, 4, 3, 2, 1))
 
     def mine(o, at):
         return ob[o * 2 + x, at, :].astype(F32) + xr[o, at, :].astype(F32)
 
-    def uo_copy(o):
-        return remote(us.at[o], ur.at[o], u_s.at[o], u_r.at[o], p + 2, q)
-
-    def do_copy(o):
-        return remote(ds.at[o], dr.at[o], d_s.at[o], d_r.at[o], p - 2, q)
-
-    def pass_on(o, first, buf, got, copy):
+    def whole(c):
+        return pl.ds(pl.multiple_of(c * CB, 16), CB)
+
+    def uo_copy(o, c):
+        return remote(us.at[o, whole(c)], ur.at[o, whole(c)], u_s.at[o, c], u_r.at[o, c], p + 2, q)
+
+    def do_copy(o, c):
+        return remote(ds.at[o, whole(c)], dr.at[o, whole(c)], d_s.at[o, c], d_r.at[o, c], p - 2, q)
+
+    def in_chunk(c, body):
+        def one(i, carry):
+            body(pl.ds(pl.multiple_of(c * CB + i * cut, 16), cut))
+            return carry
+
+        lax.fori_loop(0, CB // cut, one, 0)
+
+    def pass_on(o, c, first, buf, got, copy):
         @pl.when(first)
         def _():
             def body(at):
                 buf[o, at, :] = mine(o, at)
 
-            by_chunks(block, cut, body)
+            in_chunk(c, body)
 
         @pl.when(jnp.logical_not(first))
         def _():
-            copy(o).wait_recv()
+            copy(o, c).wait_recv()
 
             def body(at):
                 buf[o, at, :] = mine(o, at) + got[o, at, :]
 
-            by_chunks(block, cut, body)
-
-        copy(o).start()
-
-    for k in range(Z - 1):
-        hi, lo = Z - 1 - k, k
-        pl.when(z < hi)(lambda: pass_on(hi, z == 0, us, ur, uo_copy))
-        pl.when(z > lo)(lambda: pass_on(lo, z == Z - 1, ds, dr, do_copy))
-
-    def total(at):
-        out_ref[at, :] = mine(z, at)
-
-    by_chunks(block, cut, total)
-
-    @pl.when(z > 0)
-    def _():
-        uo_copy(z).wait_recv()
-
-        def body(at):
-            out_ref[at, :] += ur[z, at, :]
-
-        by_chunks(block, cut, body)
-
-    @pl.when(z < Z - 1)
-    def _():
-        do_copy(z).wait_recv()
-
-        def body(at):
-            out_ref[at, :] += dr[z, at, :]
-
-        by_chunks(block, cut, body)
+            in_chunk(c, body)
+
+        copy(o, c).start()
+
+    for n in range(NC + Z):
+        if n < NC:
+            lax.fori_loop(n * per, (n + 1) * per, out_pairs, 0)
+            for o in order:
+                xo_copy(o, n).start()
+        if 0 <= n - 1 < NC:
+            for o in order:
+                xo_copy(o, n - 1).wait_recv()
+        cu = n - 1 - z
+        cd = n - 1 - (Z - 1 - z)
+        for k in range(Z - 1):
+            hi, lo = Z - 1 - k, k
+            pl.when((z < hi) & (cu >= 0) & (cu < NC))(lambda: pass_on(hi, cu, z == 0, us, ur, uo_copy))
+            pl.when((z > lo) & (cd >= 0) & (cd < NC))(lambda: pass_on(lo, cd, z == Z - 1, ds, dr, do_copy))
+
+    for c in range(NC):
+        def total(at):
+            out_ref[at, :] = mine(z, at)
+
+        in_chunk(c, total)
+
+        @pl.when(z > 0)
+        def _():
+            uo_copy(z, c).wait_recv()
+
+            def body(at):
+                out_ref[at, :] += ur[z, at, :]
+
+            in_chunk(c, body)
+
+        @pl.when(z < Z - 1)
+        def _():
+            do_copy(z, c).wait_recv()
+
+            def body(at):
+                out_ref[at, :] += dr[z, at, :]
+
+            in_chunk(c, body)
 
     c_copy(0).wait_send()
     c_copy(1).wait_send()
@@ -536,9 +580,10 @@
     e_c.wait_send()
     e_f.wait_send()
     for o in range(Z):
-        xo_copy(o).wait_send()
-        pl.when(z < o)(lambda: uo_copy(o).wait_send())
-        pl.when(z > o)(lambda: do_copy(o).wait_send())
+        for c in range(NC):
+            xo_copy(o, c).wait_send()
+            pl.when(z < o)(lambda: uo_copy(o, c).wait_send())
+            pl.when(z > o)(lambda: do_copy(o, c).wait_send())
 
 
 def fused(readings, spectra, stiffness):
@@ -554,10 +599,12 @@
     vm = pl.BlockSpec(memory_space=pltpu.VMEM)
     dma = pltpu.SemaphoreType.DMA
     share = points * T
+    pairs = sens // 2
+    NC = best_unroll(pairs // best_unroll(pairs, (5, 4, 3, 2, 1)), (5, 4, 3, 2, 1))
     out = pl.pallas_call(
         functools.partial(kernel, (P, S, sens, rows, R)),
         out_shape=jax.ShapeDtypeStruct((block, NCOL), F32),
-        in_specs=[vm, vm, pl.BlockSpec(memory_space=pltpu.SMEM), vm, vm, vm],
+        in_specs=[vm, pl.BlockSpec(memory_space=pl.ANY), pl.BlockSpec(memory_space=pltpu.SMEM), vm, vm, vm],
         out_specs=vm,
         scratch_shapes=[
             pltpu.VMEM((P, block, NCOL), BF),
@@ -581,10 +628,11 @@
             pltpu.VMEM((Z, block, NCOL), F32),
             pltpu.VMEM((Z, block, NCOL), F32),
             pltpu.VMEM((Z, block, NCOL), F32),
-            dma((Z,)), dma((Z,)), dma((Z,)), dma((Z,)), dma((Z,)),
+            pltpu.VMEM(spectra.shape, BF), dma,
+            dma((Z, NC)), dma((Z, NC)), dma((Z, NC)), dma((Z, NC)), dma((Z, NC)),
             dma((2,)), dma((2,)), dma((1,)), dma((1,)),
             dma((2, 2)), dma((2, 2)), dma((3,)), dma((3,)),
-            dma((Z,)), dma((Z,)), dma((Z,)), dma((Z,)), dma((Z,)), dma((Z,)),
+            dma((Z, NC)), dma((Z, NC)), dma((Z, NC)), dma((Z, NC)), dma((Z, NC)), dma((Z, NC)),
         ],
         compiler_params=pltpu.CompilerParams(
             collective_id=0, has_side_effects=True, vmem_limit_bytes=60 * 2**20

time: 243 us -> 200 us (0.82)
  Pallas kernels: 236 us -> 193 us
    pallas_call x1, Pallas kernels: 236 us -> 193 us  [fused(): pl.pallas_call(functools.partial(kernel, (P, S, sens, rows, R)), out_shap...]
where the time goes in v1:
time: 200 us
  Pallas kernels  193 us (96%)
  local copies, waits for them, and re-layouts  7.22 us (4%)
    pallas_call x1, Pallas kernels, fused(): pl.pallas_call(functools.partial(kernel, (P, S, sens, rows, R)), out_shap...  193 us
    unnamed x2, local copies, waits for them, and re-layouts  7.22 us

profile of v1, /device:TPU:0, one launch (start us, length us, event | category | flops | bytes accessed | tf_op | source)
XLA Modules:
  0.0 200.3 jit_solution(8787648654100763540)
XLA Ops:
  0.0 5.3 %copy.7.spec_hbm = bf16[2,65,150,128]{3,2,1,0:T(8,128)(2,1)} copy(bf16[2,65,150,128]{3,0,2,1:T(2,128)(2,1)} %param.7) | data formatting | bytes 9984000 | tf_op args[1]
  5.3 193.0 %shard_map.64 = f32[1200,128]{1,0:T(8,128)} custom-call(bf16[1200,128]{1,0:T(8,128)(2,1)} %bitcast.7, bf16[2,65,150,128]{3,2,1,0:T(8,128)(2,1)} %copy.7.spec_hbm, f32[128]{0:T(128)} %stiff_ref.1, bf16[288,256]{1,0:T(8,128)(2,1)} %constant.6.clone.pair_ref, bf16[144,128]{1,0:T(8,128)(2,1)} %constant.7.clone.fwd_ref, bf16[64,432]{1,0:T(8,128)(2,1)} %constant.8.clone.inv_ref), custom_call_target="tpu_custom_call" | custom-call | tf_op jit(solution)/shard_map/pallas_call | solution.py:604
  198.3 1.9 copy.9

commit v2 on v1

--- a/solution.py
+++ b/solution.py
@@ -118,6 +118,7 @@
 
 
 MESH = pl.DeviceIdType.MESH
+KG = 4
 BF = jnp.bfloat16
 F32 = jnp.float32
 
@@ -326,95 +327,84 @@
 
     lax.fori_loop(0, bins, adjoint, 0)
 
-    um = best_unroll(points, (4, 2, 1))
-
-    def field_points(i, carry):
+    GC = GY // KG
+    group = R * GC
+    um = best_unroll(GC, (4, 2, 1))
+    size = group * T
+    seg = GC * T
+    step = best_unroll(size, (128, 64, 32, 16))
+
+    def span(c):
+        return pl.ds(c * size, size)
+
+    def chunk_points(c, body):
+        def one(i, carry):
+            first = i * um
+            body(c * group + first, (first // GC) * GY + c * GC + lax.rem(first, GC))
+            return carry
+
+        lax.fori_loop(0, group // um, one, 0)
+
+    def tile(i):
+        return pl.ds(pl.multiple_of(i * T, T), T)
+
+    def field_points(place, point):
         parts = []
         for j in range(um):
-            at = pl.ds(i * um + j, rows, points)
+            at = pl.ds(point + j, rows, points)
             parts.append(jnp.concatenate([are[at, :], aim[at, :]], 0))
         got = dot(inv_ref[...], three(jnp.concatenate(parts, 1)))
         for j in range(um):
             for k in range(S):
-                to = pl.ds(pl.multiple_of((i * um + j) * T, T), T)
-                fq[k, to, :] = got[k * T:(k + 1) * T, j * NCOL:(j + 1) * NCOL].astype(fq.dtype)
-        return carry
-
-    lax.fori_loop(0, points // um, field_points, 0)
-
-    share = points * T
-    step = 128
-
-    def c_copy(yy):
-        return remote(fq.at[yy * 2 + 1 - core], cr.at[yy], c_s.at[yy], c_r.at[yy], p, qc)
-
-    c_copy(1 - y).start()
-    c_copy(y).start()
-    c_copy(1 - y).wait_recv()
-
-    def sum_other(at):
-        ys[at, :] = (fq[qy, at, :].astype(F32) + cr[1 - y, at, :].astype(F32)).astype(BF)
-
-    by_chunks(share, step, sum_other)
-    y_copy = remote(ys, yr, y_s.at[0], y_r.at[0], p, qy)
-    y_copy.start()
-    c_copy(y).wait_recv()
-
-    def sum_own(at):
-        sh[at, :] = fq[q, at, :].astype(F32) + cr[y, at, :].astype(F32)
-
-    by_chunks(share, step, sum_own)
-    y_copy.wait_recv()
-
-    def sum_y(at):
-        got = sh[at, :] + yr[at, :].astype(F32)
-        sh[at, :] = got
-        hb[0, at, :] = got.astype(BF)
-
-    by_chunks(share, step, sum_y)
-
-    line = GY * T
-
-    def to_low(s):
-        return remote(hb.at[s, pl.ds(0, line)], hh.at[s], h_s.at[s, 0], h_r.at[s, 0], p - 1, q)
-
-    def to_high(s):
-        return remote(hb.at[s, pl.ds((R - 1) * line, line)], hl.at[s], h_s.at[s, 1], h_r.at[s, 1], p + 1, q)
-
-    for s in range(2):
+                fq[k, tile(place + j), :] = got[k * T:(k + 1) * T, j * NCOL:(j + 1) * NCOL]
+
+    def model_points(place, point):
+        parts = []
+        for j in range(um):
+            parts.append(jnp.concatenate([sg[k, tile(place + j), :] for k in range(S)], 0))
+        block_in = jnp.concatenate(parts, 1)
+        got = dot(fwd_ref[...], jnp.concatenate([block_in, block_in], 0))
+        for j in range(um):
+            to = pl.ds(point + j, rows, points)
+            cols = slice(j * NCOL, (j + 1) * NCOL)
+            are[to, :] = got[:rows, cols]
+            aim[to, :] = got[rows:, cols]
+
+    def c_copy(yy, c):
+        return remote(fq.at[yy * 2 + 1 - core, span(c)], cr.at[yy, span(c)], c_s.at[yy, c], c_r.at[yy, c], p, qc)
+
+    def y_copy(c):
+        return remote(ys.at[span(c)], yr.at[span(c)], y_s.at[c], y_r.at[c], p, qy)
+
+    def to_low(s, c):
+        return remote(hb.at[s, pl.ds(c * size, seg)], hh.at[s, pl.ds(c * seg, seg)],
+                      h_s.at[s, 0, c], h_r.at[s, 0, c], p - 1, q)
+
+    def to_high(s, c):
+        return remote(hb.at[s, pl.ds(c * size + (R - 1) * seg, seg)], hl.at[s, pl.ds(c * seg, seg)],
+                      h_s.at[s, 1, c], h_r.at[s, 1, c], p + 1, q)
+
+    def send_halos(s, c):
+        pl.when(p > 0)(lambda: to_low(s, c).start())
+        pl.when(p < P - 1)(lambda: to_high(s, c).start())
+
+    def sweep(s, c):
         src = sh if s == 0 else sh2
-        pl.when(p > 0)(lambda: to_low(s).start())
-        pl.when(p < P - 1)(lambda: to_high(s).start())
-
-        @pl.when(p > 0)
-        def _():
-            to_high(s).wait_recv()
-
-        @pl.when(p == 0)
-        def _():
-            hl[s] = jnp.zeros((line, NCOL), BF)
-
-        @pl.when(p < P - 1)
-        def _():
-            to_low(s).wait_recv()
-
-        @pl.when(p == P - 1)
-        def _():
-            hh[s] = jnp.zeros((line, NCOL), BF)
+        pl.when(p > 0)(lambda: to_high(s, c).wait_recv())
+        pl.when(p < P - 1)(lambda: to_low(s, c).wait_recv())
+
+        def cell(r, g):
+            return tile((g // GC) * group + r * GC + lax.rem(g, GC))
 
         def grid_column(g, carry):
             left = jnp.where(g > 0, 1.0, 0.0)
             right = jnp.where(g < GY - 1, 1.0, 0.0)
-
-            def cell(r, c):
-                return pl.ds(pl.multiple_of(r * line + c * T, T), T)
-
+            before, after = jnp.maximum(g - 1, 0), jnp.minimum(g + 1, GY - 1)
             for r in range(R):
                 here = src[cell(r, g), :]
-                side = left * src[cell(r, jnp.maximum(g - 1, 0)), :]
-                side = side + right * src[cell(r, jnp.minimum(g + 1, GY - 1)), :]
-                low = hl[s, cell(0, g), :].astype(F32) if r == 0 else src[cell(r - 1, g), :]
-                high = hh[s, cell(0, g), :].astype(F32) if r == R - 1 else src[cell(r + 1, g), :]
+                side = left * src[cell(r, before), :] + right * src[cell(r, after), :]
+                low = hl[s, tile(g), :].astype(F32) if r == 0 else src[cell(r - 1, g), :]
+                high = hh[s, tile(g), :].astype(F32) if r == R - 1 else src[cell(r + 1, g), :]
                 new = here + stiff_ref[r * GY + g] * (low + high + side - 4.0 * here)
                 if s == 0:
                     sh2[cell(r, g), :] = new
@@ -423,34 +413,79 @@
                     sg[q, cell(r, g), :] = new.astype(BF)
             return carry
 
-        lax.fori_loop(0, GY, grid_column, 0)
-
-    e_y = remote(sg.at[q], sg.at[q], e_s.at[0], e_r.at[0], p, qy)
-    e_c = remote(sg.at[q], sg.at[q], e_s.at[1], e_r.at[1], p, qc)
-    e_f = remote(sg.at[qy], sg.at[qy], e_s.at[2], e_r.at[2], p, qc)
-    e_y.start()
-    e_c.start()
-    remote(sg.at[qy], sg.at[qy], e_s.at[0], e_r.at[0], p, qy).wait_recv()
-    e_f.start()
-    remote(sg.at[qc], sg.at[qc], e_s.at[1], e_r.at[1], p, qc).wait_recv()
+        lax.fori_loop(c * GC, (c + 1) * GC, grid_column, 0)
+
     diag = (1 - y) * 2 + 1 - core
-    remote(sg.at[diag], sg.at[diag], e_s.at[2], e_r.at[2], p, qc).wait_recv()
-
-    def model_points(i, carry):
-        parts = []
-        for j in range(um):
-            at = pl.ds(pl.multiple_of((i * um + j) * T, T), T)
-            parts.append(jnp.concatenate([sg[k, at, :] for k in range(S)], 0))
-        block_in = jnp.concatenate(parts, 1)
-        got = dot(fwd_ref[...], jnp.concatenate([block_in, block_in], 0))
-        for j in range(um):
-            to = pl.ds(i * um + j, rows, points)
-            cols = slice(j * NCOL, (j + 1) * NCOL)
-            are[to, :] = got[:rows, cols]
-            aim[to, :] = got[rows:, cols]
-        return carry
-
-    lax.fori_loop(0, points // um, model_points, 0)
+
+    def e_copy(kind, origin, target, c):
+        at = sg.at[origin, span(c)]
+        return remote(at, at, e_s.at[kind, c], e_r.at[kind, c], p, target)
+
+    def at_chunk(c, body):
+        def one(i, carry):
+            body(pl.ds(pl.multiple_of(c * size + i * step, step), step))
+            return carry
+
+        lax.fori_loop(0, size // step, one, 0)
+
+    for s in range(2):
+        @pl.when(p == 0)
+        def _():
+            hl[s] = jnp.zeros((GY * T, NCOL), BF)
+
+        @pl.when(p == P - 1)
+        def _():
+            hh[s] = jnp.zeros((GY * T, NCOL), BF)
+
+    for n in range(KG + 9):
+        if n < KG:
+            chunk_points(n, field_points)
+            c_copy(1 - y, n).start()
+            c_copy(y, n).start()
+        c = n - 1
+        if 0 <= c < KG:
+            c_copy(1 - y, c).wait_recv()
+
+            def sum_other(at):
+                ys[at, :] = (fq[qy, at, :] + cr[1 - y, at, :]).astype(BF)
+
+            at_chunk(c, sum_other)
+            y_copy(c).start()
+            c_copy(y, c).wait_recv()
+
+            def sum_own(at):
+                sh[at, :] = fq[q, at, :] + cr[y, at, :]
+
+            at_chunk(c, sum_own)
+        c = n - 2
+        if 0 <= c < KG:
+            y_copy(c).wait_recv()
+
+            def sum_y(at):
+                got = sh[at, :] + yr[at, :].astype(F32)
+                sh[at, :] = got
+                hb[0, at, :] = got.astype(BF)
+
+            at_chunk(c, sum_y)
+            send_halos(0, c)
+        c = n - 4
+        if 0 <= c < KG:
+            sweep(0, c)
+            send_halos(1, c)
+        c = n - 6
+        if 0 <= c < KG:
+            sweep(1, c)
+            e_copy(0, q, qy, c).start()
+            e_copy(1, q, qc, c).start()
+        c = n - 7
+        if 0 <= c < KG:
+            e_copy(0, qy, qy, c).wait_recv()
+            e_copy(2, qy, qc, c).start()
+        c = n - 9
+        if 0 <= c < KG:
+            e_copy(1, qc, qc, c).wait_recv()
+            e_copy(2, diag, qc, c).wait_recv()
+            chunk_points(c, model_points)
 
     def forward_bin(f, carry):
         at = pl.ds(pl.multiple_of(f * points, 8), points)
@@ -570,15 +605,16 @@
 
             in_chunk(c, body)
 
-    c_copy(0).wait_send()
-    c_copy(1).wait_send()
-    y_copy.wait_send()
-    for s in range(2):
-        pl.when(p > 0)(lambda: to_low(s).wait_send())
-        pl.when(p < P - 1)(lambda: to_high(s).wait_send())
-    e_y.wait_send()
-    e_c.wait_send()
-    e_f.wait_send()
+    for c in range(KG):
+        c_copy(0, c).wait_send()
+        c_copy(1, c).wait_send()
+        y_copy(c).wait_send()
+        for s in range(2):
+            pl.when(p > 0)(lambda: to_low(s, c).wait_send())
+            pl.when(p < P - 1)(lambda: to_high(s, c).wait_send())
+        e_copy(0, q, qy, c).wait_send()
+        e_copy(1, q, qc, c).wait_send()
+        e_copy(2, qy, qc, c).wait_send()
     for o in range(Z):
         for c in range(NC):
             xo_copy(o, c).wait_send()
@@ -630,8 +666,8 @@
             pltpu.VMEM((Z, block, NCOL), F32),
             pltpu.VMEM(spectra.shape, BF), dma,
             dma((Z, NC)), dma((Z, NC)), dma((Z, NC)), dma((Z, NC)), dma((Z, NC)),
-            dma((2,)), dma((2,)), dma((1,)), dma((1,)),
-            dma((2, 2)), dma((2, 2)), dma((3,)), dma((3,)),
+            dma((2, KG)), dma((2, KG)), dma((KG,)), dma((KG,)),
+            dma((2, 2, KG)), dma((2, 2, KG)), dma((3, KG)), dma((3, KG)),
             dma((Z, NC)), dma((Z, NC)), dma((Z, NC)), dma((Z, NC)), dma((Z, NC)), dma((Z, NC)),
         ],
         compiler_params=pltpu.CompilerParams(

time: 200 us -> 174 us (0.87)
  Pallas kernels: 193 us -> 167 us
    pallas_call x1, Pallas kernels: 193 us -> 167 us  [fused(): pl.pallas_call(functools.partial(kernel, (P, S, sens, rows, R)), out_shap...]
where the time goes in v2:
time: 174 us
  Pallas kernels  167 us (96%)
  local copies, waits for them, and re-layouts  7.22 us (4%)
    pallas_call x1, Pallas kernels, fused(): pl.pallas_call(functools.partial(kernel, (P, S, sens, rows, R)), out_shap...  167 us
    unnamed x2, local copies, waits for them, and re-layouts  7.22 us

profile of v2, /device:TPU:0, one launch (start us, length us, event | category | flops | bytes accessed | tf_op | source)
XLA Modules:
  0.0 174.1 jit_solution(14916446669443779608)
XLA Ops:
  0.0 5.3 %copy.7.spec_hbm = bf16[2,65,150,128]{3,2,1,0:T(8,128)(2,1)} copy(bf16[2,65,150,128]{3,0,2,1:T(2,128)(2,1)} %param.7) | data formatting | bytes 9984000 | tf_op args[1]
  5.3 166.9 %shard_map.64 = f32[1200,128]{1,0:T(8,128)} custom-call(bf16[1200,128]{1,0:T(8,128)(2,1)} %bitcast.7, bf16[2,65,150,128]{3,2,1,0:T(8,128)(2,1)} %copy.7.spec_hbm, f32[128]{0:T(128)} %stiff_ref.1, bf16[288,256]{1,0:T(8,128)(2,1)} %constant.6.clone.pair_ref, bf16[144,128]{1,0:T(8,128)(2,1)} %constant.7.clone.fwd_ref, bf16[64,432]{1,0:T(8,128)(2,1)} %constant.8.clone.inv_ref), custom_call_target="tpu_custom_call" | custom-call | tf_op jit(solution)/shard_map/pallas_call | solution.py:640
  172.2 1.9 %copy.9 = f32[8,150,128]{2,0,1:T(8,128)} copy(f32[8,150,128]{2,0,1:T(8,128)} %bitcast.6) | data formatting | bytes 1228800
